TPU v7x, 32 devices: a whole 2x2x4 slice. The times are simulated.
32 devices in a mesh: ep: 4 (over y, x), dp: 8 (over z, core).
Axes of the slice: x: 2, y: 2, z: 4, core: 2. Of those that a mesh axis runs over, the one named last changes fastest.
Arguments:
- checkpoint: bfloat16 [4096, 2048], P('ep', 'dp'), may hold values from -6 to 6
- cotangent: bfloat16 [4096, 2048], P(('ep', 'dp')), may hold values from -6 to 6
- routes: int32 [4096, 2], P(('ep', 'dp')), may hold values from 0 to 3, all different within a row; in each aligned block of 128 rows (0 to 127, 128 to 255, ...) at most 128 rows name the same one
- gates: float32 [4096, 2], P(('ep', 'dp')), may hold values from 0.1 to 1
- w_gate: bfloat16 [4, 2048, 1024], P('ep'), may hold values from -0.125 to 0.125
- w_up: bfloat16 [4, 2048, 1024], P('ep'), may hold values from -0.125 to 0.125
- w_down: bfloat16 [4, 2048, 1024], P('ep'), may hold values from -0.1875 to 0.1875
Outputs:
- layer_out: bfloat16 [4096, 2048], P(('ep', 'dp'))
- grad_input: bfloat16 [4096, 2048], P(('ep', 'dp'))
- grad_gates: float32 [4096, 2], P(('ep', 'dp'))
- grad_w_gate: float32 [4, 2048, 1024], P('ep', 'dp')
- grad_w_up: float32 [4, 2048, 1024], P('ep', 'dp')
- grad_w_down: float32 [4, 2048, 1024], P('ep', 'dp')
Inputs may be any that keep to these rules, and one draw needn't show every extreme that they name: `routes`: among the 128 rows of one device, no expert is named by more than 128 rows, and in every draw some expert is named by exactly 128 of them; a token names 2 different experts.
All inputs are finite; a program needn't handle non-finite values.
Results may differ from a plain program's by a relative error of at most 0.022.
Values may be sent and summed in bfloat16 or wider, within the bound.
A program may use at most 128 MiB of HBM per device.

v0:
```python
import jax
import jax.numpy as jnp
from jax import lax
from jax.sharding import PartitionSpec as P


def shards(checkpoint, cotangent, routes, gates, w_gate, w_up, w_down):
    tok_rows = cotangent.shape[0]
    features = cotangent.shape[1]
    top_count = routes.shape[1]
    local_experts = w_gate.shape[0]
    hidden_units = w_gate.shape[2]
    ep_size = lax.axis_size("ep")
    experts_all = local_experts * ep_size
    capacity = tok_rows * top_count * 2 // experts_all
    pair_count = tok_rows * top_count
    gathered = lax.all_gather(checkpoint, "dp", axis=1, tiled=True)
    inputs = lax.dynamic_slice_in_dim(gathered, lax.axis_index("dp") * tok_rows, tok_rows, 0)
    flat_routes = routes.reshape(-1)
    one_hot = (flat_routes[:, None] == jnp.arange(experts_all, dtype=jnp.int32)[None, :]).astype(
        jnp.int32
    )
    slot_index = jnp.sum(jnp.cumsum(one_hot, axis=0) * one_hot, axis=1) - 1
    position = flat_routes * capacity + slot_index
    source = jnp.full((experts_all * capacity,), pair_count, jnp.int32)
    source = source.at[position].set(jnp.arange(pair_count, dtype=jnp.int32))
    token_index = jnp.minimum(source // top_count, tok_rows)
    x_padded = jnp.concatenate([inputs, jnp.zeros((1, features), jnp.bfloat16)], axis=0)
    grad_out = (gates[:, :, None] * cotangent[:, None, :].astype(jnp.float32)).astype(jnp.bfloat16)
    grad_padded = jnp.concatenate(
        [grad_out.reshape(pair_count, features), jnp.zeros((1, features), jnp.bfloat16)], axis=0
    )
    x_send = x_padded[token_index].reshape(ep_size, local_experts, capacity, features)
    d_send = grad_padded[source].reshape(ep_size, local_experts, capacity, features)
    expert_x_rows = lax.all_to_all(x_send, "ep", split_axis=0, concat_axis=0, tiled=True)
    expert_d_rows = lax.all_to_all(d_send, "ep", split_axis=0, concat_axis=0, tiled=True)
    pre_gate = jnp.einsum(
        "sxnd,xdf->sxnf", expert_x_rows, w_gate, preferred_element_type=jnp.float32
    )
    pre_up = jnp.einsum("sxnd,xdf->sxnf", expert_x_rows, w_up, preferred_element_type=jnp.float32)
    activated = jax.nn.silu(pre_gate)
    expert_hidden = (activated * pre_up).astype(jnp.bfloat16)
    outputs = jnp.einsum(
        "sxnf,xdf->sxnd", expert_hidden, w_down, preferred_element_type=jnp.float32
    ).astype(jnp.bfloat16)
    hidden_grad = jnp.einsum(
        "sxnd,xdf->sxnf", expert_d_rows, w_down, preferred_element_type=jnp.float32
    )
    sigmoid_gate = jax.nn.sigmoid(pre_gate)
    expert_gate_grad = (
        hidden_grad * pre_up * sigmoid_gate * (1.0 + pre_gate * (1.0 - sigmoid_gate))
    ).astype(jnp.bfloat16)
    expert_up_grad = (hidden_grad * activated).astype(jnp.bfloat16)
    input_part = (
        jnp.einsum("sxnf,xdf->sxnd", expert_gate_grad, w_gate, preferred_element_type=jnp.float32)
        + jnp.einsum("sxnf,xdf->sxnd", expert_up_grad, w_up, preferred_element_type=jnp.float32)
    ).astype(jnp.bfloat16)
    outputs, input_part, hidden, gate_grad, up_grad, x_rows, d_rows = (
        outputs,
        input_part,
        expert_hidden,
        expert_gate_grad,
        expert_up_grad,
        expert_x_rows,
        expert_d_rows,
    )
    returned_out, returned_part = (
        lax.all_to_all(outputs, "ep", split_axis=0, concat_axis=0, tiled=True),
        lax.all_to_all(input_part, "ep", split_axis=0, concat_axis=0, tiled=True),
    )

    def term_of(left, right):
        return jnp.einsum("sxnd,sxnf->dxf", left, right, preferred_element_type=jnp.float32)

    summed = lax.psum_scatter(
        jnp.concatenate(
            [term_of(x_rows, gate_grad), term_of(x_rows, up_grad), term_of(d_rows, hidden)], axis=2
        ).astype(jnp.bfloat16),
        "dp",
        scatter_dimension=0,
        tiled=True,
    ).astype(jnp.float32)
    summed = jnp.transpose(summed, (1, 0, 2))
    grad_w_gate = summed[:, :, :hidden_units]
    grad_w_up = summed[:, :, hidden_units : 2 * hidden_units]
    grad_w_down = summed[:, :, 2 * hidden_units :]
    out_flat = returned_out.reshape(experts_all * capacity, features)
    part_flat = returned_part.reshape(experts_all * capacity, features)
    expert_out = out_flat[position].reshape(tok_rows, top_count, features).astype(jnp.float32)
    input_parts = part_flat[position].reshape(tok_rows, top_count, features).astype(jnp.float32)
    layer_out = jnp.sum(gates[:, :, None] * expert_out, axis=1).astype(jnp.bfloat16)
    grad_gates = jnp.sum(cotangent.astype(jnp.float32)[:, None, :] * expert_out, axis=-1)
    grad_input = jnp.sum(input_parts, axis=1).astype(jnp.bfloat16)
    return (layer_out, grad_input, grad_gates, grad_w_gate, grad_w_up, grad_w_down)


def solution(mesh):
    in_specs = (
        P("ep", "dp"),
        P(("ep", "dp"), None),
        P(("ep", "dp"), None),
        P(("ep", "dp"), None),
        P("ep", None, None),
        P("ep", None, None),
        P("ep", None, None),
    )
    out_specs = (
        P(("ep", "dp"), None),
        P(("ep", "dp"), None),
        P(("ep", "dp"), None),
        P("ep", "dp", None),
        P("ep", "dp", None),
        P("ep", "dp", None),
    )
    return jax.shard_map(shards, mesh=mesh, in_specs=in_specs, out_specs=out_specs, check_vma=False)
```

profile of v0, /device:TPU:0, one launch (start us, length us, event | category | flops | bytes accessed | tf_op | source)
XLA Modules:
  0.0 276.3 jit_solution(9755756358968249970)
XLA Ops:
  11.1 2.5 mul.92
  19.1 3.3 %gather_fusion.2 = bf16[512,2048]{1,0:T(8,128)(2,1)} fusion(bf16[257,2048]{1,0:T(8,128)(2,1)S(1)} %concatenate.19, s32[1024]{0:T(1024)S(1)} %pad_clamp_fusion), kind=kCustom, calls=%fused_computation.2 | custom fusion | bytes 4196352 | tf_op jit(solution)/shard_map/gather | solution.py:34
  22.4 5.2 %all-to-all-start.2 = ((bf16[4,1,128,2048]{3,2,1,0:T(8,128)(2,1)}), bf16[4,1,128,2048]{3,2,1,0:T(8,128)(2,1)S(1)}, u32[]{:S(2)}, u32[]{:S(2)}) async-start(bf16[4,1,128,2048]{3,2,1,0:T(8,128)(2,1)} %bitcast.28), calls=%async_computation.2 | async-start | bytes 4194304 | tf_op jit(solution)/shard_map/all_to_all | solution.py:36
  27.6 32.6 %all-gather.2.cloned.1.call-done = bf16[1024,2048]{1,0:T(8,128)(2,1)} async-done(((bf16[1024,256]{1,0:T(8,128)(2,1)}), bf16[1024,2048]{1,0:T(8,128)(2,1)}) %all-gather.2.cloned.1.call-update) | async-done | bytes 4194320 | tf_op jit(solution)/shard_map/all_gather | solution.py:17
  61.3 3.3 %gather_fusion = bf16[512,2048]{1,0:T(8,128)(2,1)} fusion(bf16[129,2048]{1,0:T(8,128)(2,1)S(1)} %concatenate.18, s32[1024]{0:T(1024)S(1)} %pad_clamp_fusion.2), kind=kCustom, calls=%fused_computation | custom fusion | bytes 4196352 | tf_op jit(solution)/shard_map/gather | solution.py:33
  64.6 4.4 %all-to-all-start = ((bf16[4,1,128,2048]{3,2,1,0:T(8,128)(2,1)}), bf16[4,1,128,2048]{3,2,1,0:T(8,128)(2,1)}, u32[]{:S(2)}, u32[]{:S(2)}) async-start(bf16[4,1,128,2048]{3,2,1,0:T(8,128)(2,1)} %bitcast.5), calls=%async_computation | async-start | bytes 4194304 | tf_op jit(solution)/shard_map/all_to_all | solution.py:35
  69.3 5.8 %fusion = f32[4,128,1024]{2,1,0:T(8,128)} fusion(bf16[1,2048,1024]{2,1,0:T(8,128)(2,1)} %param.13, bf16[4,1,128,2048]{3,2,1,0:T(8,128)(2,1)S(1)} %all-to-all-done.2), kind=kOutput, calls=%fused_computation.9 | convolution fusion | flops 2147483648 | bytes 8388608 | tf_op jit(solution)/shard_map/sxnd,xdf->sxnf/dot_general | solution.py:46
  75.1 19.6 %all-to-all-done = bf16[4,1,128,2048]{3,2,1,0:T(8,128)(2,1)} async-done(((bf16[4,1,128,2048]{3,2,1,0:T(8,128)(2,1)}), bf16[4,1,128,2048]{3,2,1,0:T(8,128)(2,1)}, u32[]{:S(2)}, u32[]{:S(2)}) %all-to-all-start) | async-done | bytes 2097184 | tf_op jit(solution)/shard_map/all_to_all | solution.py:35
  94.7 5.3 %fusion.6 = f32[4,128,1024]{2,1,0:T(8,128)S(1)} fusion(bf16[1,2048,1024]{2,1,0:T(8,128)(2,1)} %param.12, bf16[4,1,128,2048]{3,2,1,0:T(8,128)(2,1)} %all-to-all-done), kind=kOutput, calls=%fused_computation.15 | convolution fusion | flops 2147483648 | bytes 8388608 | tf_op jit(solution)/shard_map/sxnd,xdf->sxnf/dot_general | solution.py:40
  100.0 4.8 %fusion.28 = (bf16[4,1,128,1024]{3,2,0,1:T(8,128)(2,1)S(1)}, bf16[4,128,1024]{2,1,0:T(8,128)(2,1)S(1)}, bf16[4,128,1024]{2,1,0:T(8,128)(2,1)S(1)}) fusion(f32[4,128,1024]{2,1,0:T(8,128)S(1)} %copy-done.11, f32[4,128,1024]{2,1,0:T(8,128)S(1)} %fusion.6, bf16[1,2048,1024]{2,1,0:T(8,128)(2,1)S(1)} %copy-done.4, bf16[4,1,128,2048]{3,2,1,0:T(8,128)(2,1)} %all-to-all-done), kind=kOutput, calls=%fused_computation.32 | convolution fusion | flops 2155347968 | bytes 13631488 | tf_op jit(solution)/shard_map/sxnd,xdf->sxnf/dot_general | solution.py:37
  107.2 4.0 %fusion.13 = bf16[2048,1,1024]{0,2,1:T(8,128)(2,1)S(1)} fusion(bf16[4,128,1024]{2,1,0:T(8,128)(2,1)S(1)} %get-tuple-element.28, bf16[4,1,128,2048]{3,2,1,0:T(8,128)(2,1)} %all-to-all-done), kind=kOutput, calls=%fused_computation.23 | convolution fusion | flops 2149580800 | bytes 7340032 | tf_op jit(solution)/shard_map/sxnd,sxnf->dxf/dot_general | solution.py:73
  111.2 4.2 %fusion.12 = bf16[2048,1,1024]{0,2,1:T(8,128)(2,1)S(1)} fusion(bf16[4,1,128,2048]{3,2,1,0:T(8,128)(2,1)} %all-to-all-done, bf16[4,1,128,1024]{3,2,0,1:T(8,128)(2,1)S(1)} %get-tuple-element.26), kind=kOutput, calls=%fused_computation.22 | convolution fusion | flops 2149580800 | bytes 7340032 | tf_op jit(solution)/shard_map/sxnd,sxnf->dxf/dot_general | solution.py:73
  115.5 21.0 %pad_maximum_fusion = bf16[2048,1,3072]{0,2,1:T(8,128)(2,1)} fusion(bf16[2048,1,1024]{0,2,1:T(8,128)(2,1)S(1)} %fusion.14, bf16[2048,1,1024]{0,2,1:T(8,128)(2,1)S(1)} %fusion.13, bf16[2048,1,1024]{0,2,1:T(8,128)(2,1)S(1)} %fusion.12), kind=kLoop, calls=%fused_computation.5 | loop fusion | flops 37748736 | bytes 25165824 | tf_op jit(solution)/shard_map/concatenate | solution.py:76
  137.7 5.9 %fusion.23 = bf16[4,1,128,2048]{3,2,1,0:T(8,128)(2,1)} fusion(bf16[4,128,1024]{2,1,0:T(8,128)(2,1)S(1)} %copy-done.10, bf16[1,2048,1024]{2,1,0:T(8,128)(2,1)} %param.13), kind=kOutput, calls=%fused_computation.27 | convolution fusion | flops 2148532224 | bytes 7340032 | tf_op jit(solution)/shard_map/sxnf,xdf->sxnd/dot_general | solution.py:43
  143.6 3.6 %all-to-all-start.1 = ((bf16[4,1,128,2048]{3,2,1,0:T(8,128)(2,1)}), bf16[4,1,128,2048]{3,2,1,0:T(8,128)(2,1)S(1)}, u32[]{:S(2)}, u32[]{:S(2)}) async-start(bf16[4,1,128,2048]{3,2,1,0:T(8,128)(2,1)} %fusion.23), calls=%async_computation.1 | async-start | bytes 4194304 | tf_op jit(solution)/shard_map/all_to_all | solution.py:68
  147.3 5.1 %fusion.4 = f32[4,128,2048]{2,1,0:T(8,128)S(1)} fusion(bf16[4,128,1024]{2,1,0:T(8,128)(2,1)} %copy-done.6, bf16[1,2048,1024]{2,1,0:T(8,128)(2,1)} %param.12), kind=kOutput, calls=%fused_computation.13 | convolution fusion | flops 2147483648 | bytes 9437184 | tf_op jit(solution)/shard_map/sxnf,xdf->sxnd/dot_general | solution.py:56
  152.4 3.7 %fusion.20 = bf16[4,1,128,2048]{3,2,1,0:T(8,128)(2,1)} fusion(f32[4,128,2048]{2,1,0:T(8,128)S(1)} %fusion.4, bf16[1,2048,1024]{2,1,0:T(8,128)(2,1)S(1)} %copy-done.5, bf16[4,1,128,1024]{3,2,0,1:T(8,128)(2,1)S(1)} %copy-done.8), kind=kOutput, calls=%fused_computation.26 | convolution fusion | flops 2149580800 | bytes 11534336 | tf_op jit(solution)/shard_map/sxnf,xdf->sxnd/dot_general | solution.py:55
  156.1 15.8 %all-to-all-done.1 = bf16[4,1,128,2048]{3,2,1,0:T(8,128)(2,1)S(1)} async-done(((bf16[4,1,128,2048]{3,2,1,0:T(8,128)(2,1)}), bf16[4,1,128,2048]{3,2,1,0:T(8,128)(2,1)S(1)}, u32[]{:S(2)}, u32[]{:S(2)}) %all-to-all-start.1) | async-done | bytes 2097184 | tf_op jit(solution)/shard_map/all_to_all | solution.py:68
  171.9 4.7 %all-to-all-start.3 = ((bf16[4,1,128,2048]{3,2,1,0:T(8,128)(2,1)}), bf16[4,1,128,2048]{3,2,1,0:T(8,128)(2,1)}, u32[]{:S(2)}, u32[]{:S(2)}) async-start(bf16[4,1,128,2048]{3,2,1,0:T(8,128)(2,1)} %fusion.20), calls=%async_computation.3 | async-start | bytes 4194304 | tf_op jit(solution)/shard_map/all_to_all | solution.py:69
  180.5 20.6 %all-to-all-done.3 = bf16[4,1,128,2048]{3,2,1,0:T(8,128)(2,1)} async-done(((bf16[4,1,128,2048]{3,2,1,0:T(8,128)(2,1)}), bf16[4,1,128,2048]{3,2,1,0:T(8,128)(2,1)}, u32[]{:S(2)}, u32[]{:S(2)}) %all-to-all-start.3) | async-done | bytes 2097184 | tf_op jit(solution)/shard_map/all_to_all | solution.py:69
  201.1 4.2 %gather_fusion.3 = bf16[256,2048]{1,0:T(8,128)(2,1)S(1)} fusion(bf16[512,2048]{1,0:T(8,128)(2,1)} %bitcast.43, s32[1024]{0:T(1024)S(1)} %pad_clamp_fusion.1), kind=kCustom, calls=%fused_computation.3 | custom fusion | bytes 2098176 | tf_op jit(solution)/shard_map/gather | solution.py:90
  206.8 4.6 %reduce_sum.41 = bf16[128,2048]{1,0:T(8,128)(2,1)} reduce(bf16[128,2,2048]{2,1,0:T(2,128)(2,1)} %reshape.200, bf16[]{:T(256)} %constant.20.clone.1), dimensions={1}, to_apply=%region_5.6 | reduce | flops 262144 | bytes 1572866 | tf_op jit(solution)/shard_map/reduce_sum | solution.py:93
  211.5 4.9 %multiply_reduce_fusion = (f32[128,2]{1,0:T(8,128)S(1)}, bf16[128,2048]{1,0:T(8,128)(2,1)}) fusion(f32[128,2,2048]{2,1,0:T(2,128)S(1)} %reshape.201, f32[128,2048]{1,0:T(8,128)S(1)} %copy-done, f32[128,2]{1,0:T(8,128)S(1)} %copy.35), kind=kLoop, calls=%fused_computation.49 | loop fusion | flops 1834752 | bytes 3672064 | tf_op jit(solution)/shard_map/reduce_sum | solution.py:92
  217.0 46.2 %reduce-scatter.2.cloned.1.call-done = bf16[256,1,3072]{0,2,1:T(8,128)(2,1)} async-done(((bf16[2048,1,3072]{0,2,1:T(8,128)(2,1)}), bf16[256,1,3072]{0,2,1:T(8,128)(2,1)}) %reduce-scatter.2.cloned.1.call-update) | async-done | bytes 1572880 | tf_op jit(solution)/shard_map/reduce_scatter | solution.py:75
  (70 shorter events, 26.0 us)
Async XLA Ops:
  7.2 53.0 %all-gather.2.cloned.1.call-start = ((), (), s32[]{:S(2)}) async-start(), calls=%async_computation.5 | async-start | bytes 4718592 | tf_op jit(solution)/shard_map/all_gather | solution.py:17
  11.1 2.5 copy-start.3
  11.1 2.8 copy-start.2
  22.4 42.2 %all-to-all-start.2 = ((bf16[4,1,128,2048]{3,2,1,0:T(8,128)(2,1)}), bf16[4,1,128,2048]{3,2,1,0:T(8,128)(2,1)S(1)}, u32[]{:S(2)}, u32[]{:S(2)}) async-start(bf16[4,1,128,2048]{3,2,1,0:T(8,128)(2,1)} %bitcast.28), calls=%async_computation.2 | async-start | bytes 4194304 | tf_op jit(solution)/shard_map/all_to_all | solution.py:36
  64.6 30.1 %all-to-all-start = ((bf16[4,1,128,2048]{3,2,1,0:T(8,128)(2,1)}), bf16[4,1,128,2048]{3,2,1,0:T(8,128)(2,1)}, u32[]{:S(2)}, u32[]{:S(2)}) async-start(bf16[4,1,128,2048]{3,2,1,0:T(8,128)(2,1)} %bitcast.5), calls=%async_computation | async-start | bytes 4194304 | tf_op jit(solution)/shard_map/all_to_all | solution.py:35
  69.1 194.1 %reduce-scatter.2.cloned.1.call-start = ((), (), s32[]{:S(2)}) async-start(), calls=%async_computation.6 | async-start | bytes 14155776 | tf_op jit(solution)/shard_map/reduce_scatter | solution.py:75
  94.7 5.3 %copy-start.4 = (bf16[1,2048,1024]{2,1,0:T(8,128)(2,1)S(1)}, bf16[1,2048,1024]{2,1,0:T(8,128)(2,1)}, u32[]{:S(2)}) copy-start(bf16[1,2048,1024]{2,1,0:T(8,128)(2,1)} %param.11) | copy-start | bytes 12582916
  94.7 5.3 %copy-start.11 = (f32[4,128,1024]{2,1,0:T(8,128)S(1)}, f32[4,128,1024]{2,1,0:T(8,128)}, u32[]{:S(2)}) copy-start(f32[4,128,1024]{2,1,0:T(8,128)} %fusion) | copy-start | bytes 6291460
  104.8 2.4 copy-start.9
  104.8 2.4 copy-start.6
  104.8 6.4 %copy-start.7 = (bf16[4,1,128,1024]{3,2,0,1:T(8,128)(2,1)}, bf16[4,1,128,1024]{3,2,0,1:T(8,128)(2,1)S(1)}, u32[]{:S(2)}) copy-start(bf16[4,1,128,1024]{3,2,0,1:T(8,128)(2,1)S(1)} %get-tuple-element.26) | copy-start | bytes 3145732
  136.5 1.2 copy-start.10
  143.6 28.3 %all-to-all-start.1 = ((bf16[4,1,128,2048]{3,2,1,0:T(8,128)(2,1)}), bf16[4,1,128,2048]{3,2,1,0:T(8,128)(2,1)S(1)}, u32[]{:S(2)}, u32[]{:S(2)}) async-start(bf16[4,1,128,2048]{3,2,1,0:T(8,128)(2,1)} %fusion.23), calls=%async_computation.1 | async-start | bytes 4194304 | tf_op jit(solution)/shard_map/all_to_all | solution.py:68
  147.3 5.1 %copy-start.5 = (bf16[1,2048,1024]{2,1,0:T(8,128)(2,1)S(1)}, bf16[1,2048,1024]{2,1,0:T(8,128)(2,1)}, u32[]{:S(2)}) copy-start(bf16[1,2048,1024]{2,1,0:T(8,128)(2,1)} %param.11) | copy-start | bytes 12582916
  147.3 5.1 %copy-start.8 = (bf16[4,1,128,1024]{3,2,0,1:T(8,128)(2,1)S(1)}, bf16[4,1,128,1024]{3,2,0,1:T(8,128)(2,1)}, u32[]{:S(2)}) copy-start(bf16[4,1,128,1024]{3,2,0,1:T(8,128)(2,1)} %copy-done.7) | copy-start | bytes 3145732
  156.1 20.5 %copy-start.1 = (bf16[128,2048]{1,0:T(8,128)(2,1)S(1)}, bf16[128,2048]{1,0:T(8,128)(2,1)}, u32[]{:S(2)}) copy-start(bf16[128,2048]{1,0:T(8,128)(2,1)} %param.8) | copy-start | bytes 1572868
  171.9 29.2 %all-to-all-start.3 = ((bf16[4,1,128,2048]{3,2,1,0:T(8,128)(2,1)}), bf16[4,1,128,2048]{3,2,1,0:T(8,128)(2,1)}, u32[]{:S(2)}, u32[]{:S(2)}) async-start(bf16[4,1,128,2048]{3,2,1,0:T(8,128)(2,1)} %fusion.20), calls=%async_computation.3 | async-start | bytes 4194304 | tf_op jit(solution)/shard_map/all_to_all | solution.py:69
  206.8 4.6 %copy-start = (f32[128,2048]{1,0:T(8,128)S(1)}, f32[128,2048]{1,0:T(8,128)}, u32[]{:S(2)}) copy-start(f32[128,2048]{1,0:T(8,128)} %convert_element_type.81) | copy-start | bytes 3145732
Sparse Core Ops, SparseCore 0:
  9.6 50.5 all-gather.1
  136.6 126.5 reduce-scatter.1
where the time goes:
time: 282 us; the launch traced here: 276 us
  waiting for transfers between devices  135 us (48%)
  matrix products  41.2 us (15%)
  other arithmetic  36.5 us (13%)
  local copies, waits for them, and re-layouts  30.1 us (11%)
  starting transfers between devices  18.2 us (6%)
  between operations  14.8 us (5%)
    reduce_scatter x1, waiting for transfers between devices, shards(): lax.psum_scatter(jnp.concatenate([term_of(x_rows, gate_grad), term_of(x_r...  46.2 us
    all_gather x1, waiting for transfers between devices, shards(): gathered = lax.all_gather(checkpoint, 'dp', axis=1, tiled=True)  32.6 us
    concatenate x1, other arithmetic, shards(): jnp.concatenate([term_of(x_rows, gate_grad), term_of(x_rows, up_grad), te...  21 us
    all_to_all x1, waiting for transfers between devices, shards(): lax.all_to_all(input_part, 'ep', split_axis=0, concat_axis=0, tiled=True)  20.6 us
    all_to_all x1, waiting for transfers between devices, shards(): lax.all_to_all(x_send, 'ep', split_axis=0, concat_axis=0, tiled=True)  19.6 us
    all_to_all x1, waiting for transfers between devices, shards(): lax.all_to_all(outputs, 'ep', split_axis=0, concat_axis=0, tiled=True)  15.8 us
    dot_general x3, matrix products, term_of(): jnp.einsum('sxnd,sxnf->dxf', left, right, preferred_element_type=jnp.floa...  10.6 us
    unnamed x30, local copies, waits for them, and re-layouts  6.71 us
  transfers between devices with their start and end apart: 6, of which 5 were waited for; matrix products, arithmetic and copies ran while one was open for 21% of the time, Pallas kernels for 0%

commit v1 on v0

v1 whole, which is shorter than its diff:
```python
import jax
import jax.numpy as jnp
from jax import lax
from jax.sharding import PartitionSpec as P

F32 = jnp.float32
BF16 = jnp.bfloat16


def dot(left, right, left_dim, right_dim):
    return lax.dot_general(
        left, right, (((left_dim,), (right_dim,)), ((), ())), preferred_element_type=F32
    )


def shards(checkpoint, cotangent, routes, gates, w_gate, w_up, w_down):
    tok_rows, features = cotangent.shape
    ep_size = lax.axis_size("ep")
    w_gate, w_up, w_down = w_gate[0], w_up[0], w_down[0]

    chosen = routes[:, :, None] == jnp.arange(ep_size, dtype=jnp.int32)[None, None, :]
    gate_table = jnp.sum(jnp.where(chosen, gates[:, :, None], 0.0), axis=1)
    gate = lax.all_to_all(gate_table.T, "ep", split_axis=0, concat_axis=0, tiled=True)
    gate = gate.reshape(ep_size * tok_rows, 1)
    cot = lax.all_gather(cotangent, "ep", axis=0, tiled=True)
    inputs = lax.all_to_all(checkpoint, "dp", split_axis=0, concat_axis=1, tiled=True)
    x = lax.all_gather(inputs, "ep", axis=0, tiled=True)

    hidden_back = dot(cot, w_down, 1, 0)
    pre_gate = dot(x, w_gate, 1, 0)
    pre_up = dot(x, w_up, 1, 0)
    sigmoid = jax.nn.sigmoid(pre_gate)
    activated = pre_gate * sigmoid
    hidden = activated * pre_up
    gated_hidden = (gate * hidden).astype(BF16)
    gate_dots = jnp.sum(hidden_back * hidden, axis=1)
    hidden_grad = gate * hidden_back
    gate_grad = (hidden_grad * pre_up * sigmoid * (1.0 + pre_gate * (1.0 - sigmoid))).astype(BF16)
    up_grad = (hidden_grad * activated).astype(BF16)

    def scattered(left, right):
        term = dot(left, right, 0, 0).astype(BF16)
        summed = lax.psum_scatter(term, "dp", scatter_dimension=0, tiled=True)
        return summed.astype(F32)[None]

    grad_w_down = scattered(cot, gated_hidden)
    grad_w_gate = scattered(x, gate_grad)
    grad_w_up = scattered(x, up_grad)

    def returned(rows):
        rows = rows.reshape(ep_size, tok_rows, -1)
        return lax.all_to_all(rows, "ep", split_axis=0, concat_axis=0, tiled=True)

    gate_dots = returned(gate_dots)[:, :, 0]
    out_part = returned(dot(gated_hidden, w_down, 1, 1).astype(BF16))
    in_part = returned((dot(gate_grad, w_gate, 1, 1) + dot(up_grad, w_up, 1, 1)).astype(BF16))
    layer_out = jnp.sum(out_part.astype(F32), axis=0).astype(BF16)
    grad_input = jnp.sum(in_part.astype(F32), axis=0).astype(BF16)
    grad_gates = jnp.sum(jnp.where(chosen, gate_dots.T[:, None, :], 0.0), axis=2)
    return (layer_out, grad_input, grad_gates, grad_w_gate, grad_w_up, grad_w_down)


def solution(mesh):
    tokens = P(("ep", "dp"), None)
    weights = P("ep", None, None)
    slices = P("ep", "dp", None)
    return jax.shard_map(
        shards,
        mesh=mesh,
        in_specs=(P("ep", "dp"), tokens, tokens, tokens, weights, weights, weights),
        out_specs=(tokens, tokens, tokens, slices, slices, slices),
        check_vma=False,
    )
```

time: 282 us -> 290 us (1.028); the launches traced: 276 us -> 289 us
  blocking collectives: 0 us -> 35.9 us
  waiting for transfers between devices: 135 us -> 166 us
  other arithmetic: 36.5 us -> 10.7 us
  local copies, waits for them, and re-layouts: 30.1 us -> 9.61 us
  starting transfers between devices: 18.2 us -> 8.46 us
  matrix products: 41.2 us -> 44.6 us
    all_to_all x0 -> x3, blocking collectives: none -> 35.9 us  [the longest x1 21.7 us: shards(): lax.all_to_all(checkpoint, 'dp', split_axis=0, concat_axis=1, tiled=True)]
    all_gather x1 -> x2, waiting for transfers between devices: 32.6 us -> 61.6 us  [the longest x1 33.4 us: shards(): x = lax.all_gather(inputs, 'ep', axis=0, tiled=True)]
    concatenate x1 -> x0, other arithmetic: 21 us -> none  [shards(): jnp.concatenate([term_of(x_rows, gate_grad), term_of(x_rows, up_grad), te...]
    reduce_scatter x1 -> x3, waiting for transfers between devices: 46.2 us -> 66.4 us  [scattered(): summed = lax.psum_scatter(term, 'dp', scatter_dimension=0, tiled=True)]
    all_to_all x4 -> x2, waiting for transfers between devices: 56 us -> 37.3 us  [returned(): return lax.all_to_all(rows, 'ep', split_axis=0, concat_axis=0, tiled=True)]
    gather x4 -> x0, local copies, waits for them, and re-layouts: 12.2 us -> none  [the longest x1 4.22 us: shards(): part_flat[position].reshape(tok_rows, top_count, features)]
    all_to_all x4 -> x2, starting transfers between devices: 17.9 us -> 8.08 us  [returned(): return lax.all_to_all(rows, 'ep', split_axis=0, concat_axis=0, tiled=True)]
    mul x5 -> x0, local copies, waits for them, and re-layouts: 4.96 us -> none  [the longest x2 4.57 us: shards(): gates[:, :, None] * cotangent[:, None, :].astype(jnp.float32)]
  transfers between devices with their start and end apart: 6 -> 7, of which waited for: 5 -> 6; matrix products, arithmetic and copies ran while one was open for 21% -> 15% of each run, Pallas kernels for 0% -> 0%
where the time goes in v1:
time: 290 us; the launch traced here: 289 us
  waiting for transfers between devices  166 us (57%)
  matrix products  44.6 us (15%)
  blocking collectives  35.9 us (12%)
  between operations  13.9 us (5%)
  other arithmetic  10.7 us (4%)
  local copies, waits for them, and re-layouts  9.61 us (3%)
  starting transfers between devices  8.46 us (3%)
    reduce_scatter x3, waiting for transfers between devices, scattered(): summed = lax.psum_scatter(term, 'dp', scatter_dimension=0, tiled=True)  66.4 us
    dot_general x9, matrix products, dot(): lax.dot_general(left, right, (((left_dim,), (right_dim,)), ((), ())), pre...  44.6 us
    all_to_all x2, waiting for transfers between devices, returned(): return lax.all_to_all(rows, 'ep', split_axis=0, concat_axis=0, tiled=True)  37.3 us
    all_gather x1, waiting for transfers between devices, shards(): x = lax.all_gather(inputs, 'ep', axis=0, tiled=True)  33.4 us
    all_gather x1, waiting for transfers between devices, shards(): cot = lax.all_gather(cotangent, 'ep', axis=0, tiled=True)  28.2 us
    all_to_all x1, blocking collectives, shards(): lax.all_to_all(checkpoint, 'dp', split_axis=0, concat_axis=1, tiled=True)  21.7 us
    unnamed x25, local copies, waits for them, and re-layouts  8.61 us
    all_to_all x2, starting transfers between devices, returned(): return lax.all_to_all(rows, 'ep', split_axis=0, concat_axis=0, tiled=True)  8.08 us
  transfers between devices with their start and end apart: 7, of which 6 were waited for; matrix products, arithmetic and copies ran while one was open for 15% of the time, Pallas kernels for 0%

profile of v1, /device:TPU:0, one launch (start us, length us, event | category | flops | bytes accessed | tf_op | source)
XLA Modules:
  0.0 289.2 jit_solution(13252999616900195862)
XLA Ops:
  7.2 21.7 %all_to_all.43 = bf16[8,128,256]{2,1,0:T(8,128)(2,1)S(1)} all-to-all(bf16[8,128,256]{2,1,0:T(8,128)(2,1)} %bitcast.69), channel_id=1, replica_groups=mesh['ep'=4,'dp'=8] {'dp'}, dimensions={0} | all-to-all | bytes 1048576 | tf_op jit(solution)/shard_map/all_to_all | solution.py:26
  30.7 33.4 %all-gather.3.cloned.1.call-done = bf16[512,2048]{0,1:T(8,128)(2,1)} async-done(((bf16[128,2048]{0,1:T(8,128)(2,1)}), bf16[512,2048]{0,1:T(8,128)(2,1)}) %all-gather.3.cloned.1.call-update) | async-done | bytes 2097168 | tf_op jit(solution)/shard_map/all_gather | solution.py:27
  64.2 5.3 %fusion.6 = f32[512,1024]{1,0:T(8,128)S(1)} fusion(bf16[512,2048]{0,1:T(8,128)(2,1)} %all-gather.3.cloned.1.call-done, bf16[1,2048,1024]{2,1,0:T(8,128)(2,1)} %param.12), kind=kOutput, calls=%fused_computation.6 | convolution fusion | flops 2147483648 | bytes 8388608 | tf_op jit(solution)/shard_map/dot_general | solution.py:11
  69.5 3.7 %fusion.10 = f32[512,1024]{1,0:T(8,128)} fusion(bf16[512,2048]{0,1:T(8,128)(2,1)S(1)} %copy-done.8, bf16[1,2048,1024]{2,1,0:T(8,128)(2,1)S(1)} %copy-done.6), kind=kOutput, calls=%fused_computation.10 | convolution fusion | flops 2147483648 | bytes 8388608 | tf_op jit(solution)/shard_map/dot_general | solution.py:11
  73.2 28.2 %all-gather.5.cloned.1.call-done = bf16[512,2048]{1,0:T(8,128)(2,1)} async-done(((bf16[128,2048]{1,0:T(8,128)(2,1)}), bf16[512,2048]{1,0:T(8,128)(2,1)}) %all-gather.5.cloned.1.call-update) | async-done | bytes 2097168 | tf_op jit(solution)/shard_map/all_gather | solution.py:25
  101.4 6.2 %multiply_reduce_fusion = (f32[512]{0:T(512)S(1)}, f32[512,1024]{1,0:T(8,128)S(1)}) fusion(f32[512,1024]{1,0:T(8,128)S(1)} %fusion.6, f32[512,1024]{1,0:T(8,128)} %fusion.10, bf16[512,2048]{1,0:T(8,128)(2,1)} %all-gather.5.cloned.1.call-done, bf16[1,2048,1024]{2,1,0:T(8,128)(2,1)} %param.13), kind=kOutput, calls=%fused_computation.17 | convolution fusion | flops 2151153152 | bytes 12584960 | tf_op jit(solution)/shard_map/dot_general | solution.py:11
  107.6 7.2 %all_to_all.44 = f32[4,128,1]{1,2,0:T(1,128)S(1)} all-to-all(f32[4,128,1]{1,2,0:T(1,128)S(1)} %bitcast.73), channel_id=1, replica_groups=mesh['ep'=4,'dp'=8] {'ep'}, dimensions={0} | all-to-all | bytes 4096 | tf_op jit(solution)/shard_map/all_to_all | solution.py:52
  115.4 7.0 %all_to_all.45 = f32[4,1,128]{2,1,0:T(1,128)S(1)} all-to-all(f32[4,1,128]{2,1,0:T(1,128)S(1)} %bitcast.72), channel_id=1, replica_groups=mesh['ep'=4,'dp'=8] {'ep'}, dimensions={0} | all-to-all | bytes 4096 | tf_op jit(solution)/shard_map/all_to_all | solution.py:23
  122.4 2.6 multiply_convert_fusion.1
  125.9 4.4 %convert_bitcast_fusion = bf16[2048,1024]{0,1:T(8,128)(2,1)} fusion(bf16[512,1024]{1,0:T(8,128)(2,1)S(1)} %get-tuple-element.40, bf16[512,2048]{1,0:T(8,128)(2,1)S(1)} %copy-done.10), kind=kOutput, calls=%fused_computation.12 | convolution fusion | flops 2149580800 | bytes 7340032 | tf_op jit(solution)/shard_map/dot_general | solution.py:11
  130.5 1.3 copy-done.9
  131.9 4.3 %convert_bitcast_fusion.2 = bf16[2048,1024]{0,1:T(8,128)(2,1)} fusion(bf16[512,1024]{1,0:T(8,128)(2,1)S(1)} %get-tuple-element.38, bf16[512,2048]{0,1:T(8,128)(2,1)S(1)} %copy-done.9), kind=kOutput, calls=%fused_computation.14 | convolution fusion | flops 2149580800 | bytes 7340032 | tf_op jit(solution)/shard_map/dot_general | solution.py:11
  137.4 6.0 %convert_bitcast_fusion.1 = bf16[2048,1024]{0,1:T(8,128)(2,1)} fusion(bf16[512,1024]{1,0:T(8,128)(2,1)S(1)} %copy-done.1, bf16[512,2048]{0,1:T(8,128)(2,1)} %all-gather.3.cloned.1.call-done), kind=kOutput, calls=%fused_computation.13 | convolution fusion | flops 2149580800 | bytes 7340032 | tf_op jit(solution)/shard_map/dot_general | solution.py:11
  144.6 5.9 %fusion.14 = bf16[512,2048]{1,0:T(8,128)(2,1)} fusion(bf16[512,1024]{1,0:T(8,128)(2,1)S(1)} %copy-done.3, bf16[1,2048,1024]{2,1,0:T(8,128)(2,1)} %param.13), kind=kOutput, calls=%fused_computation.16 | convolution fusion | flops 2148532224 | bytes 7340032 | tf_op jit(solution)/shard_map/dot_general | solution.py:11
  150.5 3.6 %all-to-all-start.2 = ((bf16[4,128,2048]{2,1,0:T(8,128)(2,1)}), bf16[4,128,2048]{2,1,0:T(8,128)(2,1)S(1)}, u32[]{:S(2)}, u32[]{:S(2)}) async-start(bf16[4,128,2048]{2,1,0:T(8,128)(2,1)} %bitcast.66), calls=%async_computation.2 | async-start | bytes 4194304 | tf_op jit(solution)/shard_map/all_to_all | solution.py:52
  154.2 5.1 %fusion.4 = f32[512,2048]{1,0:T(8,128)S(1)} fusion(bf16[512,1024]{1,0:T(8,128)(2,1)} %get-tuple-element.39, bf16[1,2048,1024]{2,1,0:T(8,128)(2,1)} %param.12), kind=kOutput, calls=%fused_computation.4 | convolution fusion | flops 2147483648 | bytes 9437184 | tf_op jit(solution)/shard_map/dot_general | solution.py:11
  159.3 3.7 %add_convert_fusion = bf16[512,2048]{1,0:T(8,128)(2,1)} fusion(f32[512,2048]{1,0:T(8,128)S(1)} %fusion.4, bf16[512,1024]{1,0:T(8,128)(2,1)S(1)} %get-tuple-element.38, bf16[1,2048,1024]{2,1,0:T(8,128)(2,1)S(1)} %copy-done.7), kind=kOutput, calls=%fused_computation.15 | convolution fusion | flops 2149580800 | bytes 11534336 | tf_op jit(solution)/shard_map/dot_general | solution.py:11
  163.0 14.1 %all-to-all-done.2 = bf16[4,128,2048]{2,1,0:T(8,128)(2,1)S(1)} async-done(((bf16[4,128,2048]{2,1,0:T(8,128)(2,1)}), bf16[4,128,2048]{2,1,0:T(8,128)(2,1)S(1)}, u32[]{:S(2)}, u32[]{:S(2)}) %all-to-all-start.2) | async-done | bytes 2097184 | tf_op jit(solution)/shard_map/all_to_all | solution.py:52
  177.1 4.5 %all-to-all-start.3 = ((bf16[4,128,2048]{2,1,0:T(8,128)(2,1)}), bf16[4,128,2048]{2,1,0:T(8,128)(2,1)}, u32[]{:S(2)}, u32[]{:S(2)}) async-start(bf16[4,128,2048]{2,1,0:T(8,128)(2,1)} %bitcast.65), calls=%async_computation.3 | async-start | bytes 4194304 | tf_op jit(solution)/shard_map/all_to_all | solution.py:52
  181.6 1.3 reduce_sum.52
  182.9 23.2 %all-to-all-done.3 = bf16[4,128,2048]{2,1,0:T(8,128)(2,1)} async-done(((bf16[4,128,2048]{2,1,0:T(8,128)(2,1)}), bf16[4,128,2048]{2,1,0:T(8,128)(2,1)}, u32[]{:S(2)}, u32[]{:S(2)}) %all-to-all-start.3) | async-done | bytes 2097184 | tf_op jit(solution)/shard_map/all_to_all | solution.py:52
  206.1 2.9 %reduce_sum.53 = bf16[128,2048]{1,0:T(8,128)(2,1)} reduce(bf16[4,128,2048]{2,1,0:T(8,128)(2,1)} %all-to-all-done.3, bf16[]{:T(256)} %constant.6.clone.1), dimensions={0}, to_apply=%region_2.3 | reduce | flops 786432 | bytes 2621442 | tf_op jit(solution)/shard_map/reduce_sum | solution.py:58
  211.4 18.5 %reduce-scatter.4.cloned.1.call-done = bf16[256,1024]{0,1:T(8,128)(2,1)} async-done(((bf16[2048,1024]{0,1:T(8,128)(2,1)}), bf16[256,1024]{0,1:T(8,128)(2,1)}) %reduce-scatter.4.cloned.1.call-update) | async-done | bytes 524304 | tf_op jit(solution)/shard_map/reduce_scatter | solution.py:43
  232.3 47.9 %reduce-scatter.6.cloned.1.call-done = bf16[256,1024]{0,1:T(8,128)(2,1)} async-done(((bf16[2048,1024]{0,1:T(8,128)(2,1)}), bf16[256,1024]{0,1:T(8,128)(2,1)}) %reduce-scatter.6.cloned.1.call-update) | async-done | bytes 524304 | tf_op jit(solution)/shard_map/reduce_scatter | solution.py:43
  (40 shorter events, 13.3 us)
Async XLA Ops:
  7.2 57.0 %all-gather.3.cloned.1.call-start = ((), (), s32[]{:S(2)}) async-start(), calls=%async_computation.8 | async-start | bytes 2621440 | tf_op jit(solution)/shard_map/all_gather | solution.py:27
  29.9 71.4 %all-gather.5.cloned.1.call-start = ((), (), s32[]{:S(2)}) async-start(), calls=%async_computation.9 | async-start | bytes 2621440 | tf_op jit(solution)/shard_map/all_gather | solution.py:25
  30.7 178.3 %reduce-scatter.8.cloned.1.call-start = ((), (), s32[]{:S(2)}) async-start(), calls=%async_computation.12 | async-start | bytes 4718592 | tf_op jit(solution)/shard_map/reduce_scatter | solution.py:43
  64.2 5.3 %copy-start.6 = (bf16[1,2048,1024]{2,1,0:T(8,128)(2,1)S(1)}, bf16[1,2048,1024]{2,1,0:T(8,128)(2,1)}, u32[]{:S(2)}) copy-start(bf16[1,2048,1024]{2,1,0:T(8,128)(2,1)} %param.11) | copy-start | bytes 12582916
  64.2 5.3 %copy-start.8 = (bf16[512,2048]{0,1:T(8,128)(2,1)S(1)}, bf16[512,2048]{0,1:T(8,128)(2,1)}, u32[]{:S(2)}) copy-start(bf16[512,2048]{0,1:T(8,128)(2,1)} %all-gather.3.cloned.1.call-done) | copy-start | bytes 6291460
  73.2 41.6 %copy-start.4 = (s32[128,2]{0,1:T(2,128)S(1)}, s32[128,2]{0,1:T(2,128)}, u32[]{:S(2)}) copy-start(s32[128,2]{0,1:T(2,128)} %param.9) | copy-start | bytes 3076
  73.2 41.6 %copy-start.5 = (f32[128,2]{0,1:T(2,128)S(1)}, f32[128,2]{0,1:T(2,128)}, u32[]{:S(2)}) copy-start(f32[128,2]{0,1:T(2,128)} %param.10) | copy-start | bytes 3076
  101.4 21.0 %copy-start = (f32[512,1024]{1,0:T(8,128)S(1)}, f32[512,1024]{1,0:T(8,128)}, u32[]{:S(2)}) copy-start(f32[512,1024]{1,0:T(8,128)} %fusion.10) | copy-start | bytes 6291460
  122.4 3.5 %copy-start.10 = (bf16[512,2048]{1,0:T(8,128)(2,1)S(1)}, bf16[512,2048]{1,0:T(8,128)(2,1)}, u32[]{:S(2)}) copy-start(bf16[512,2048]{1,0:T(8,128)(2,1)} %all-gather.5.cloned.1.call-done) | copy-start | bytes 6291460
  124.9 1.0 copy-start.2
  130.3 1.6 copy-start.9
  130.3 99.6 %reduce-scatter.4.cloned.1.call-start = ((), (), s32[]{:S(2)}) async-start(), calls=%async_computation.10 | async-start | bytes 4718592 | tf_op jit(solution)/shard_map/reduce_scatter | solution.py:43
  136.2 1.2 copy-start.1
  136.2 144.0 %reduce-scatter.6.cloned.1.call-start = ((), (), s32[]{:S(2)}) async-start(), calls=%async_computation.11 | async-start | bytes 4718592 | tf_op jit(solution)/shard_map/reduce_scatter | solution.py:43
  143.4 1.2 copy-start.3
  150.5 26.6 %all-to-all-start.2 = ((bf16[4,128,2048]{2,1,0:T(8,128)(2,1)}), bf16[4,128,2048]{2,1,0:T(8,128)(2,1)S(1)}, u32[]{:S(2)}, u32[]{:S(2)}) async-start(bf16[4,128,2048]{2,1,0:T(8,128)(2,1)} %bitcast.66), calls=%async_computation.2 | async-start | bytes 4194304 | tf_op jit(solution)/shard_map/all_to_all | solution.py:52
  154.2 5.1 %copy-start.7 = (bf16[1,2048,1024]{2,1,0:T(8,128)(2,1)S(1)}, bf16[1,2048,1024]{2,1,0:T(8,128)(2,1)}, u32[]{:S(2)}) copy-start(bf16[1,2048,1024]{2,1,0:T(8,128)(2,1)} %param.11) | copy-start | bytes 12582916
  177.1 28.9 %all-to-all-start.3 = ((bf16[4,128,2048]{2,1,0:T(8,128)(2,1)}), bf16[4,128,2048]{2,1,0:T(8,128)(2,1)}, u32[]{:S(2)}, u32[]{:S(2)}) async-start(bf16[4,128,2048]{2,1,0:T(8,128)(2,1)} %bitcast.65), calls=%async_computation.3 | async-start | bytes 4194304 | tf_op jit(solution)/shard_map/all_to_all | solution.py:52
Sparse Core Ops, SparseCore 0:
  30.1 34.0 all-gather.2
  66.0 35.3 all-gather.4
  130.4 49.1 reduce-scatter.7
  181.7 48.1 reduce-scatter.3
  232.1 48.1 reduce-scatter.5

commit v2 on v1

v2 whole, which is shorter than its diff:
```python
import functools

import jax
import jax.numpy as jnp
from jax import lax
from jax.experimental import pallas as pl
from jax.experimental.pallas import tpu as pltpu
from jax.sharding import PartitionSpec as P

F32 = jnp.float32
BF16 = jnp.bfloat16

MESH = pl.DeviceIdType.MESH
VMEM_BYTES = 56 * 1024 * 1024
LAG = 2


def remote(src, dst, send, recv, where):
    return pltpu.make_async_remote_copy(
        src_ref=src,
        dst_ref=dst,
        send_sem=send,
        recv_sem=recv,
        device_id=where,
        device_id_type=MESH,
    )


def dispatch_kernel(
    ep, dp, saved, cot, table, x_all, cot_all, table_all, own_sem, x_send, x_recv, e_send, e_recv
):
    me_ep, me_dp = lax.axis_index("ep"), lax.axis_index("dp")
    tok, width = cot.shape[0], saved.shape[1]
    barrier = pltpu.get_barrier_semaphore()
    for i in range(1, ep):
        pl.semaphore_signal(
            barrier, inc=1, device_id={"ep": lax.rem(me_ep + i, ep)}, device_id_type=MESH
        )
    for i in range(1, dp):
        pl.semaphore_signal(
            barrier, inc=1, device_id={"dp": lax.rem(me_dp + i, dp)}, device_id_type=MESH
        )
    pl.semaphore_wait(barrier, ep + dp - 2)

    def rows(index):
        return saved.at[pl.ds(pl.multiple_of(index * tok, tok), tok), :]

    columns = x_all.at[me_ep, :, pl.ds(pl.multiple_of(me_dp * width, width), width)]
    slices = []
    for i in range(1, dp):
        to = lax.rem(me_dp + i, dp)
        slices.append(remote(rows(to), columns, x_send.at[i], x_recv.at[i], {"dp": to}))
        slices[-1].start()
    blocks = []
    for a, (src, dst) in enumerate(((cot, cot_all), (table, table_all), (x_all, x_all))):
        for i in range(1, ep):
            to = lax.rem(me_ep + i, ep)
            part = src if a == 0 else src.at[to if a == 1 else me_ep]
            blocks.append(
                remote(part, dst.at[me_ep], e_send.at[a, i], e_recv.at[a, i], {"ep": to})
            )
            if a < 2:
                blocks[-1].start()
    local = [
        pltpu.make_async_copy(rows(me_dp), columns, own_sem.at[0]),
        pltpu.make_async_copy(cot, cot_all.at[me_ep], own_sem.at[1]),
        pltpu.make_async_copy(table.at[me_ep], table_all.at[me_ep], own_sem.at[2]),
    ]
    for copy in local:
        copy.start()
    local[0].wait()
    for copy in slices:
        copy.wait_recv()
    for copy in blocks[2 * (ep - 1) :]:
        copy.start()
    for copy in slices:
        copy.wait_send()
    local[1].wait()
    local[2].wait()
    for copy in blocks:
        copy.wait()


def dispatch(checkpoint, cotangent, table, ep, dp):
    tok, features = cotangent.shape
    anywhere = pl.BlockSpec(memory_space=pl.ANY)
    rows = jax.ShapeDtypeStruct((ep, tok, features), BF16)
    return pl.pallas_call(
        functools.partial(dispatch_kernel, ep, dp),
        out_shape=(rows, rows, jax.ShapeDtypeStruct(table.shape, F32)),
        in_specs=[anywhere] * 3,
        out_specs=(anywhere,) * 3,
        scratch_shapes=[
            pltpu.SemaphoreType.DMA((3,)),
            pltpu.SemaphoreType.DMA((dp,)),
            pltpu.SemaphoreType.DMA((dp,)),
            pltpu.SemaphoreType.DMA((3, ep)),
            pltpu.SemaphoreType.DMA((3, ep)),
        ],
        compiler_params=pltpu.CompilerParams(collective_id=0, has_side_effects=True),
    )(checkpoint, cotangent, table)


def combine_kernel(ep, dp, *refs):
    sent, terms, back, sums = refs[0:3], refs[3:6], refs[6:9], refs[9:12]
    own, core, right, left = refs[12:16]
    own_sem, ret_send, ret_recv, core_send, core_recv = refs[16:21]
    right_send, right_recv, left_send, left_recv = refs[21:25]
    me_ep, me_dp = lax.axis_index("ep"), lax.axis_index("dp")
    chips = dp // 2
    z, c = me_dp // 2, lax.rem(me_dp, 2)
    partner = {"dp": z * 2 + 1 - c}
    up, down = {"dp": me_dp + 2}, {"dp": me_dp - 2}
    not_last, not_first = z < chips - 1, z > 0

    loads = []
    for m in range(3):
        loads.append(pltpu.make_async_copy(terms[m], own.at[m], own_sem.at[m]))
        loads[-1].start()
    barrier = pltpu.get_barrier_semaphore()
    for i in range(1, ep):
        pl.semaphore_signal(
            barrier, inc=1, device_id={"ep": lax.rem(me_ep + i, ep)}, device_id_type=MESH
        )
    pl.semaphore_signal(barrier, inc=1, device_id=partner, device_id_type=MESH)

    @pl.when(not_last)
    def _():
        pl.semaphore_signal(barrier, inc=1, device_id=up, device_id_type=MESH)

    @pl.when(not_first)
    def _():
        pl.semaphore_signal(barrier, inc=1, device_id=down, device_id_type=MESH)

    pl.semaphore_wait(barrier, ep + not_last.astype(jnp.int32) + not_first.astype(jnp.int32))

    def core_copy(d, m):
        return remote(
            own.at[m, d * 2 + 1 - c], core.at[d, m], core_send.at[d, m], core_recv.at[d, m], partner
        )

    def right_copy(d, m):
        return remote(
            core.at[d, m], right.at[d, m], right_send.at[d, m], right_recv.at[d, m], up
        )

    def left_copy(d, m):
        return remote(core.at[d, m], left.at[d, m], left_send.at[d, m], left_recv.at[d, m], down)

    for copy in loads:
        copy.wait()
    lower = z < chips // 2
    for k in range(chips):
        for m in range(3):
            core_copy(jnp.where(lower, chips - 1 - k, k), m).start()

    returns = []
    for a in range(3):
        for i in range(1, ep):
            to = lax.rem(me_ep + i, ep)
            returns.append(
                remote(
                    sent[a].at[to],
                    back[a].at[me_ep],
                    ret_send.at[a, i],
                    ret_recv.at[a, i],
                    {"ep": to},
                )
            )
            returns[-1].start()
    keeps = [
        pltpu.make_async_copy(sent[a].at[me_ep], back[a].at[me_ep], own_sem.at[3 + a])
        for a in range(3)
    ]
    for copy in keeps:
        copy.start()

    steps = (chips - 1) * 3
    right_lag = jnp.where(lower, 0, LAG)
    left_lag = LAG - right_lag

    def step(i, carry):
        ir, il = i - right_lag, i - left_lag
        kr, mr = lax.div(jnp.maximum(ir, 0), 3), lax.rem(jnp.maximum(ir, 0), 3)
        kl, ml = lax.div(jnp.maximum(il, 0), 3), lax.rem(jnp.maximum(il, 0), 3)
        dr, dl = chips - 1 - kr, kl

        def forward(d, m, mine, arrived, copy_of, has):
            @pl.when(mine)
            def _():
                core_copy(d, m).wait_recv()

                @pl.when(has)
                def _():
                    copy_of(d, m).wait_recv()
                    core[d, m] = (
                        own[m, d * 2 + c].astype(F32)
                        + core[d, m].astype(F32)
                        + arrived[d, m].astype(F32)
                    ).astype(BF16)

                @pl.when(jnp.logical_not(has))
                def _():
                    core[d, m] = (
                        own[m, d * 2 + c].astype(F32) + core[d, m].astype(F32)
                    ).astype(BF16)

                copy_of(d, m).start()

        forward(dr, mr, (ir >= 0) & (ir < steps) & (dr > z), right, right_copy, not_first)
        forward(dl, ml, (il >= 0) & (il < steps) & (dl < z), left, left_copy, not_last)
        return carry

    lax.fori_loop(0, steps + LAG, step, 0)

    for m in range(3):
        core_copy(z, m).wait_recv()
        sums[m][...] = own[m, z * 2 + c].astype(F32) + core[z, m].astype(F32)

        @pl.when(not_first)
        def _():
            right_copy(z, m).wait_recv()
            sums[m][...] += right[z, m].astype(F32)

        @pl.when(not_last)
        def _():
            left_copy(z, m).wait_recv()
            sums[m][...] += left[z, m].astype(F32)

    for d in range(chips):
        for m in range(3):
            core_copy(d, m).wait_send()

            @pl.when(d > z)
            def _():
                right_copy(d, m).wait_send()

            @pl.when(d < z)
            def _():
                left_copy(d, m).wait_send()

    for copy in keeps + returns:
        copy.wait()


def combine(sent, terms, ep, dp):
    features, units = terms[0].shape
    rows, chips = features // dp, dp // 2
    anywhere = pl.BlockSpec(memory_space=pl.ANY)
    dma = pltpu.SemaphoreType.DMA
    slots = pltpu.VMEM((chips, 3, rows, units), BF16)
    return pl.pallas_call(
        functools.partial(combine_kernel, ep, dp),
        out_shape=[jax.ShapeDtypeStruct(a.shape, a.dtype) for a in sent]
        + [jax.ShapeDtypeStruct((rows, units), F32)] * 3,
        in_specs=[anywhere] * 6,
        out_specs=[anywhere] * 3 + [pl.BlockSpec(memory_space=pltpu.VMEM)] * 3,
        scratch_shapes=[pltpu.VMEM((3, dp, rows, units), BF16), slots, slots, slots, dma((6,))]
        + [dma((3, ep))] * 2
        + [dma((chips, 3))] * 6,
        compiler_params=pltpu.CompilerParams(
            collective_id=1, has_side_effects=True, vmem_limit_bytes=VMEM_BYTES
        ),
    )(*sent, *[term.reshape(dp, rows, units) for term in terms])


def dot(left, right, left_dim, right_dim):
    return lax.dot_general(
        left, right, (((left_dim,), (right_dim,)), ((), ())), preferred_element_type=F32
    )


def shards(checkpoint, cotangent, routes, gates, w_gate, w_up, w_down):
    tok_rows, features = cotangent.shape
    ep_size = lax.axis_size("ep")
    w_gate, w_up, w_down = w_gate[0], w_up[0], w_down[0]

    chosen = routes[:, :, None] == jnp.arange(ep_size, dtype=jnp.int32)[None, None, :]
    gate_table = jnp.sum(jnp.where(chosen, gates[:, :, None], 0.0), axis=1)
    table = jnp.broadcast_to(gate_table.T[:, None, :], (ep_size, 8, tok_rows))
    x, cot, table = dispatch(checkpoint, cotangent, table, ep_size, lax.axis_size("dp"))
    x, cot = (rows.reshape(ep_size * tok_rows, features) for rows in (x, cot))
    gate = table[:, 0, :].reshape(ep_size * tok_rows, 1)

    hidden_back = dot(cot, w_down, 1, 0)
    pre_gate = dot(x, w_gate, 1, 0)
    pre_up = dot(x, w_up, 1, 0)
    sigmoid = jax.nn.sigmoid(pre_gate)
    activated = pre_gate * sigmoid
    hidden = activated * pre_up
    gated_hidden = (gate * hidden).astype(BF16)
    gate_dots = jnp.sum(hidden_back * hidden, axis=1)
    hidden_grad = gate * hidden_back
    gate_grad = (hidden_grad * pre_up * sigmoid * (1.0 + pre_gate * (1.0 - sigmoid))).astype(BF16)
    up_grad = (hidden_grad * activated).astype(BF16)

    terms = [
        dot(left, right, 0, 0).astype(BF16)
        for left, right in ((x, gate_grad), (x, up_grad), (cot, gated_hidden))
    ]
    out_part = dot(gated_hidden, w_down, 1, 1).astype(BF16)
    in_part = (dot(gate_grad, w_gate, 1, 1) + dot(up_grad, w_up, 1, 1)).astype(BF16)
    out_part, in_part = (
        rows.reshape(ep_size, tok_rows, features) for rows in (out_part, in_part)
    )
    gate_dots = jnp.broadcast_to(
        gate_dots.reshape(ep_size, 1, tok_rows), (ep_size, 8, tok_rows)
    )
    out_part, in_part, gate_dots, grad_w_gate, grad_w_up, grad_w_down = combine(
        (out_part, in_part, gate_dots), terms, ep_size, lax.axis_size("dp")
    )
    gate_dots = gate_dots[:, 0, :]
    layer_out = jnp.sum(out_part.astype(F32), axis=0).astype(BF16)
    grad_input = jnp.sum(in_part.astype(F32), axis=0).astype(BF16)
    grad_gates = jnp.sum(jnp.where(chosen, gate_dots.T[:, None, :], 0.0), axis=2)
    return (
        layer_out,
        grad_input,
        grad_gates,
        grad_w_gate[None],
        grad_w_up[None],
        grad_w_down[None],
    )


def solution(mesh):
    tokens = P(("ep", "dp"), None)
    weights = P("ep", None, None)
    slices = P("ep", "dp", None)
    return jax.shard_map(
        shards,
        mesh=mesh,
        in_specs=(P("ep", "dp"), tokens, tokens, tokens, weights, weights, weights),
        out_specs=(tokens, tokens, tokens, slices, slices, slices),
        check_vma=False,
    )
```

time: 290 us -> 212 us (0.73)
  waiting for transfers between devices: 166 us -> 0 us
  Pallas kernels: 0 us -> 164 us
  blocking collectives: 35.9 us -> 0 us
  between operations: 13.9 us -> 0.73 us
  matrix products: 44.6 us -> 34.3 us
  starting transfers between devices: 8.46 us -> 0 us
  other arithmetic: 10.7 us -> 5.65 us
    pallas_call x0 -> x2, Pallas kernels: none -> 164 us  [the longest x1 110 us: combine(): pl.pallas_call(functools.partial(combine_kernel, ep, dp), out_shape=[jax....]
    reduce_scatter x3 -> x0, waiting for transfers between devices: 66.4 us -> none  [scattered(): summed = lax.psum_scatter(term, 'dp', scatter_dimension=0, tiled=True)]
    all_gather x2 -> x0, waiting for transfers between devices: 61.6 us -> none  [the longest x1 33.4 us: shards(): x = lax.all_gather(inputs, 'ep', axis=0, tiled=True)]
    all_to_all x2 -> x0, waiting for transfers between devices: 37.3 us -> none  [returned(): return lax.all_to_all(rows, 'ep', split_axis=0, concat_axis=0, tiled=True)]
    all_to_all x3 -> x0, blocking collectives: 35.9 us -> none  [the longest x1 21.7 us: shards(): lax.all_to_all(checkpoint, 'dp', split_axis=0, concat_axis=1, tiled=True)]
    dot_general x9, matrix products: 44.6 us -> 34.3 us  [dot(): lax.dot_general(left, right, (((left_dim,), (right_dim,)), ((), ())), pre...]
    all_to_all x2 -> x0, starting transfers between devices: 8.08 us -> none  [returned(): return lax.all_to_all(rows, 'ep', split_axis=0, concat_axis=0, tiled=True)]
    unnamed x25 -> x21, local copies, waits for them, and re-layouts: 8.61 us -> 4.86 us
  transfers between devices with their start and end apart: 7 -> 0, of which waited for: 6 -> 0; matrix products, arithmetic and copies ran while one was open for 15% -> 0% of each run, Pallas kernels for 0% -> 0%
where the time goes in v2:
time: 212 us
  Pallas kernels  164 us (77%)
  matrix products  34.3 us (16%)
  local copies, waits for them, and re-layouts  7.52 us (4%)
  other arithmetic  5.65 us (3%)
    pallas_call x1, Pallas kernels, combine(): pl.pallas_call(functools.partial(combine_kernel, ep, dp), out_shape=[jax....  110 us
    pallas_call x1, Pallas kernels, dispatch(): pl.pallas_call(functools.partial(dispatch_kernel, ep, dp), out_shape=(row...  53.4 us
    dot_general x9, matrix products, dot(): lax.dot_general(left, right, (((left_dim,), (right_dim,)), ((), ())), pre...  34.3 us
    unnamed x21, local copies, waits for them, and re-layouts  4.86 us

profile of v2, /device:TPU:0, one launch (start us, length us, event | category | flops | bytes accessed | tf_op | source)
XLA Modules:
  0.0 212.0 jit_solution(13336263163758396251)
XLA Ops:
  0.6 0.7 select_reduce_fusion.1
  1.3 0.6 broadcast_in_dim.50.table
  2.0 53.4 %shard_map.118 = (bf16[4,128,2048]{2,1,0:T(8,128)(2,1)}, bf16[4,128,2048]{2,1,0:T(8,128)(2,1)}, f32[4,8,128]{2,1,0:T(8,128)}) custom-call(bf16[1024,256]{1,0:T(8,128)(2,1)} %saved.1, bf16[128,2048]{1,0:T(8,128)(2,1)} %cot.1, f32[4,8,128]{2,1,0:T(8,128)} %broadcast_in_dim.50.table), custom_call_target="tpu_custom_call" | custom-call | tf_op jit(solution)/shard_map/pallas_call | solution.py:88
  55.4 0.7 slice.6
  56.1 5.3 %fusion.6 = f32[512,1024]{1,0:T(8,128)S(1)} fusion(bf16[512,2048]{1,0:T(8,128)(2,1)} %bitcast.61, bf16[1,2048,1024]{2,1,0:T(8,128)(2,1)} %param.12), kind=kOutput, calls=%fused_computation.6 | convolution fusion | flops 2147483648 | bytes 8388608 | tf_op jit(solution)/shard_map/dot_general | solution.py:268
  61.4 0.0 copy-start.4
  61.4 2.3 %fusion.10 = f32[512,1024]{1,0:T(8,128)S(1)} fusion(bf16[512,2048]{1,0:T(8,128)(2,1)S(1)} %bitcast.62, bf16[1,2048,1024]{2,1,0:T(8,128)(2,1)S(1)} %copy-done.6), kind=kOutput, calls=%fused_computation.10 | convolution fusion | flops 2147483648 | bytes 8388608 | tf_op jit(solution)/shard_map/dot_general | solution.py:268
  63.8 0.5 copy-done.8
  64.3 3.5 %multiply_reduce_fusion = (f32[512]{0:T(512)S(1)}, bf16[512,1024]{1,0:T(8,128)(2,1)S(1)}, bf16[512,1024]{1,0:T(8,128)(2,1)S(1)}, bf16[512,1024]{1,0:T(8,128)(2,1)S(1)}) fusion(f32[512,1024]{1,0:T(8,128)S(1)} %fusion.6, f32[512,1024]{1,0:T(8,128)S(1)} %fusion.10, f32[512]{0:T(512)S(1)} %bitcast.60, bf16[512,2048]{1,0:T(8,128)(2,1)S(1)} %bitcast.65, ...), kind=kOutput, calls=%fused_computation.17 | convolution fusion | flops 2157444608 | bytes 13635584 | tf_op jit(solution)/shard_map/dot_general | solution.py:268
  67.8 0.6 broadcast_in_dim.52.refs_2_
  68.4 4.4 %convolution_convert_fusion = bf16[2048,1024]{1,0:T(8,128)(2,1)} fusion(bf16[512,2048]{1,0:T(8,128)(2,1)S(1)} %bitcast.66, bf16[512,1024]{1,0:T(8,128)(2,1)S(1)} %get-tuple-element.26), kind=kOutput, calls=%fused_computation.13 | convolution fusion | flops 2149580800 | bytes 7340032 | tf_op jit(solution)/shard_map/dot_general | solution.py:268
  72.8 3.7 %fusion.14 = bf16[512,2048]{1,0:T(8,128)(2,1)} fusion(bf16[512,1024]{1,0:T(8,128)(2,1)S(1)} %get-tuple-element.26, bf16[1,2048,1024]{2,1,0:T(8,128)(2,1)S(1)} %copy-done.4), kind=kOutput, calls=%fused_computation.16 | convolution fusion | flops 2148532224 | bytes 7340032 | tf_op jit(solution)/shard_map/dot_general | solution.py:268
  76.5 4.6 %convolution_convert_fusion.2 = bf16[2048,1024]{1,0:T(8,128)(2,1)} fusion(bf16[512,2048]{1,0:T(8,128)(2,1)S(1)} %bitcast.63, bf16[512,1024]{1,0:T(8,128)(2,1)S(1)} %get-tuple-element.25), kind=kOutput, calls=%fused_computation.15 | convolution fusion | flops 2149580800 | bytes 7340032 | tf_op jit(solution)/shard_map/dot_general | solution.py:268
  81.1 4.4 %convolution_convert_fusion.1 = bf16[2048,1024]{1,0:T(8,128)(2,1)} fusion(bf16[512,2048]{1,0:T(8,128)(2,1)S(1)} %bitcast.64, bf16[512,1024]{1,0:T(8,128)(2,1)S(1)} %get-tuple-element.27), kind=kOutput, calls=%fused_computation.14 | convolution fusion | flops 2149580800 | bytes 7340032 | tf_op jit(solution)/shard_map/dot_general | solution.py:268
  85.4 2.4 %fusion.4 = f32[512,2048]{1,0:T(8,128)S(1)} fusion(bf16[512,1024]{1,0:T(8,128)(2,1)S(1)} %get-tuple-element.27, bf16[1,2048,1024]{2,1,0:T(8,128)(2,1)S(1)} %copy-done.5), kind=kOutput, calls=%fused_computation.4 | convolution fusion | flops 2147483648 | bytes 9437184 | tf_op jit(solution)/shard_map/dot_general | solution.py:268
  87.8 3.7 %add_convert_fusion = bf16[512,2048]{1,0:T(8,128)(2,1)} fusion(f32[512,2048]{1,0:T(8,128)S(1)} %fusion.4, bf16[512,1024]{1,0:T(8,128)(2,1)S(1)} %get-tuple-element.25, bf16[1,2048,1024]{2,1,0:T(8,128)(2,1)S(1)} %copy-done.6), kind=kOutput, calls=%fused_computation.12 | convolution fusion | flops 2149580800 | bytes 11534336 | tf_op jit(solution)/shard_map/dot_general | solution.py:268
  91.5 110.5 %shard_map.119 = (bf16[4,128,2048]{2,1,0:T(8,128)(2,1)}, bf16[4,128,2048]{2,1,0:T(8,128)(2,1)}, f32[4,8,128]{2,1,0:T(8,128)}, f32[256,1024]{1,0:T(8,128)}, f32[256,1024]{1,0:T(8,128)}, /*index=5*/f32[256,1024]{1,0:T(8,128)}) custom-call(bf16[4,128,2048]{2,1,0:T(8,128)(2,1)} %bitcast.52, bf16[4,128,2048]{2,1,0:T(8,128)(2,1)} %bitcast.53, ...), custom_call_target="tpu_custom_call" | custom-call | tf_op jit(solution)/shard_map/pallas_call | solution.py:252
  202.0 3.1 %reduce_sum.53 = bf16[128,2048]{1,0:T(8,128)(2,1)} reduce(bf16[4,128,2048]{2,1,0:T(8,128)(2,1)} %get-tuple-element.18, bf16[]{:T(256)} %constant.6.clone.1), dimensions={0}, to_apply=%region_2.3 | reduce | flops 786432 | bytes 2621442 | tf_op jit(solution)/shard_map/reduce_sum | solution.py:313
  205.1 1.3 reduce_sum.54
  206.4 0.7 slice.7
  207.1 0.6 select_reduce_fusion
  207.7 2.4 %copy.19 = f32[1,256,1024]{2,1,0:T(8,128)} copy(f32[1,256,1024]{2,1,0:T(8,128)} %bitcast.56) | data formatting | bytes 2097152
  210.1 1.0 copy.20
  211.1 1.0 copy.21
  (16 shorter events, 0.0 us)
Async XLA Ops:
  56.1 5.3 %copy-start.6 = (bf16[1,2048,1024]{2,1,0:T(8,128)(2,1)S(1)}, bf16[1,2048,1024]{2,1,0:T(8,128)(2,1)}, u32[]{:S(2)}) copy-start(bf16[1,2048,1024]{2,1,0:T(8,128)(2,1)} %param.11) | copy-start | bytes 12582916
  56.1 5.3 %copy-start.7 = (bf16[4,128,2048]{2,1,0:T(8,128)(2,1)S(1)}, bf16[4,128,2048]{2,1,0:T(8,128)(2,1)}, u32[]{:S(2)}) copy-start(bf16[4,128,2048]{2,1,0:T(8,128)(2,1)} %get-tuple-element.16) | copy-start | bytes 6291460
  61.4 2.4 %copy-start.4 = (bf16[1,2048,1024]{2,1,0:T(8,128)(2,1)S(1)}, bf16[1,2048,1024]{2,1,0:T(8,128)(2,1)}, u32[]{:S(2)}) copy-start(bf16[1,2048,1024]{2,1,0:T(8,128)(2,1)} %param.13) | copy-start | bytes 12582916
  61.4 2.9 %copy-start.8 = (bf16[4,128,2048]{2,1,0:T(8,128)(2,1)S(1)}, bf16[4,128,2048]{2,1,0:T(8,128)(2,1)}, u32[]{:S(2)}) copy-start(bf16[4,128,2048]{2,1,0:T(8,128)(2,1)} %get-tuple-element.17) | copy-start | bytes 6291460
  81.1 4.4 %copy-start.5 = (bf16[1,2048,1024]{2,1,0:T(8,128)(2,1)S(1)}, bf16[1,2048,1024]{2,1,0:T(8,128)(2,1)}, u32[]{:S(2)}) copy-start(bf16[1,2048,1024]{2,1,0:T(8,128)(2,1)} %param.12) | copy-start | bytes 12582916
  202.0 3.1 %copy-start = (bf16[4,128,2048]{2,1,0:T(8,128)(2,1)S(1)}, bf16[4,128,2048]{2,1,0:T(8,128)(2,1)}, u32[]{:S(2)}) copy-start(bf16[4,128,2048]{2,1,0:T(8,128)(2,1)} %get-tuple-element.19) | copy-start | bytes 6291460
  202.0 5.1 %copy-start.3 = (s32[128,2]{0,1:T(2,128)S(1)}, s32[128,2]{0,1:T(2,128)}, u32[]{:S(2)}) copy-start(s32[128,2]{0,1:T(2,128)} %param.9) | copy-start | bytes 3076
  205.1 5.0 %copy-start.2 = (f32[256,1024]{1,0:T(8,128)S(1)}, f32[256,1024]{1,0:T(8,128)}, u32[]{:S(2)}) copy-start(f32[256,1024]{1,0:T(8,128)} %get-tuple-element.22) | copy-start | bytes 3145732
  207.7 3.4 %copy-start.1 = (f32[256,1024]{1,0:T(8,128)S(1)}, f32[256,1024]{1,0:T(8,128)}, u32[]{:S(2)}) copy-start(f32[256,1024]{1,0:T(8,128)} %get-tuple-element.23) | copy-start | bytes 3145732

commit v3 on v2

--- a/solution.py
+++ b/solution.py
@@ -147,11 +147,11 @@
     def left_copy(d, m):
         return remote(core.at[d, m], left.at[d, m], left_send.at[d, m], left_recv.at[d, m], down)
 
-    for copy in loads:
-        copy.wait()
     lower = z < chips // 2
     for k in range(chips):
         for m in range(3):
+            if k == 0:
+                loads[m].wait()
             core_copy(jnp.where(lower, chips - 1 - k, k), m).start()
 
     returns = []

time: 212 us -> 211 us (level)
  no operation moved by 1% of the time
where the time goes in v3:
time: 211 us; the launch traced here: 210 us
  Pallas kernels  162 us (77%)
  matrix products  34.3 us (16%)
  local copies, waits for them, and re-layouts  7.52 us (4%)
  other arithmetic  5.65 us (3%)
    pallas_call x1, Pallas kernels, combine(): pl.pallas_call(functools.partial(combine_kernel, ep, dp), out_shape=[jax....  109 us
    pallas_call x1, Pallas kernels, dispatch(): pl.pallas_call(functools.partial(dispatch_kernel, ep, dp), out_shape=(row...  53.4 us
    dot_general x9, matrix products, dot(): lax.dot_general(left, right, (((left_dim,), (right_dim,)), ((), ())), pre...  34.3 us
    unnamed x21, local copies, waits for them, and re-layouts  4.86 us

profile of v3, /device:TPU:0, one launch (start us, length us, event | category | flops | bytes accessed | tf_op | source)
XLA Modules:
  0.0 210.2 jit_solution(12818224298763053482)
XLA Ops:
  0.6 0.7 select_reduce_fusion.1
  1.3 0.6 broadcast_in_dim.50.table
  2.0 53.4 %shard_map.118 = (bf16[4,128,2048]{2,1,0:T(8,128)(2,1)}, bf16[4,128,2048]{2,1,0:T(8,128)(2,1)}, f32[4,8,128]{2,1,0:T(8,128)}) custom-call(bf16[1024,256]{1,0:T(8,128)(2,1)} %saved.1, bf16[128,2048]{1,0:T(8,128)(2,1)} %cot.1, f32[4,8,128]{2,1,0:T(8,128)} %broadcast_in_dim.50.table), custom_call_target="tpu_custom_call" | custom-call | tf_op jit(solution)/shard_map/pallas_call | solution.py:88
  55.4 0.7 slice.6
  56.1 5.3 %fusion.6 = f32[512,1024]{1,0:T(8,128)S(1)} fusion(bf16[512,2048]{1,0:T(8,128)(2,1)} %bitcast.61, bf16[1,2048,1024]{2,1,0:T(8,128)(2,1)} %param.12), kind=kOutput, calls=%fused_computation.6 | convolution fusion | flops 2147483648 | bytes 8388608 | tf_op jit(solution)/shard_map/dot_general | solution.py:268
  61.4 2.3 %fusion.10 = f32[512,1024]{1,0:T(8,128)S(1)} fusion(bf16[512,2048]{1,0:T(8,128)(2,1)S(1)} %bitcast.62, bf16[1,2048,1024]{2,1,0:T(8,128)(2,1)S(1)} %copy-done.6), kind=kOutput, calls=%fused_computation.10 | convolution fusion | flops 2147483648 | bytes 8388608 | tf_op jit(solution)/shard_map/dot_general | solution.py:268
  63.8 0.5 copy-done.8
  64.3 3.5 %multiply_reduce_fusion = (f32[512]{0:T(512)S(1)}, bf16[512,1024]{1,0:T(8,128)(2,1)S(1)}, bf16[512,1024]{1,0:T(8,128)(2,1)S(1)}, bf16[512,1024]{1,0:T(8,128)(2,1)S(1)}) fusion(f32[512,1024]{1,0:T(8,128)S(1)} %fusion.6, f32[512,1024]{1,0:T(8,128)S(1)} %fusion.10, f32[512]{0:T(512)S(1)} %bitcast.60, bf16[512,2048]{1,0:T(8,128)(2,1)S(1)} %bitcast.65, ...), kind=kOutput, calls=%fused_computation.17 | convolution fusion | flops 2157444608 | bytes 13635584 | tf_op jit(solution)/shard_map/dot_general | solution.py:268
  67.8 0.6 broadcast_in_dim.52.refs_2_
  68.4 4.4 %convolution_convert_fusion = bf16[2048,1024]{1,0:T(8,128)(2,1)} fusion(bf16[512,2048]{1,0:T(8,128)(2,1)S(1)} %bitcast.66, bf16[512,1024]{1,0:T(8,128)(2,1)S(1)} %get-tuple-element.26), kind=kOutput, calls=%fused_computation.13 | convolution fusion | flops 2149580800 | bytes 7340032 | tf_op jit(solution)/shard_map/dot_general | solution.py:268
  72.8 3.7 %fusion.14 = bf16[512,2048]{1,0:T(8,128)(2,1)} fusion(bf16[512,1024]{1,0:T(8,128)(2,1)S(1)} %get-tuple-element.26, bf16[1,2048,1024]{2,1,0:T(8,128)(2,1)S(1)} %copy-done.4), kind=kOutput, calls=%fused_computation.16 | convolution fusion | flops 2148532224 | bytes 7340032 | tf_op jit(solution)/shard_map/dot_general | solution.py:268
  76.5 4.6 %convolution_convert_fusion.2 = bf16[2048,1024]{1,0:T(8,128)(2,1)} fusion(bf16[512,2048]{1,0:T(8,128)(2,1)S(1)} %bitcast.63, bf16[512,1024]{1,0:T(8,128)(2,1)S(1)} %get-tuple-element.25), kind=kOutput, calls=%fused_computation.15 | convolution fusion | flops 2149580800 | bytes 7340032 | tf_op jit(solution)/shard_map/dot_general | solution.py:268
  81.1 4.4 %convolution_convert_fusion.1 = bf16[2048,1024]{1,0:T(8,128)(2,1)} fusion(bf16[512,2048]{1,0:T(8,128)(2,1)S(1)} %bitcast.64, bf16[512,1024]{1,0:T(8,128)(2,1)S(1)} %get-tuple-element.27), kind=kOutput, calls=%fused_computation.14 | convolution fusion | flops 2149580800 | bytes 7340032 | tf_op jit(solution)/shard_map/dot_general | solution.py:268
  85.4 2.4 %fusion.4 = f32[512,2048]{1,0:T(8,128)S(1)} fusion(bf16[512,1024]{1,0:T(8,128)(2,1)S(1)} %get-tuple-element.27, bf16[1,2048,1024]{2,1,0:T(8,128)(2,1)S(1)} %copy-done.5), kind=kOutput, calls=%fused_computation.4 | convolution fusion | flops 2147483648 | bytes 9437184 | tf_op jit(solution)/shard_map/dot_general | solution.py:268
  87.8 3.7 %add_convert_fusion = bf16[512,2048]{1,0:T(8,128)(2,1)} fusion(f32[512,2048]{1,0:T(8,128)S(1)} %fusion.4, bf16[512,1024]{1,0:T(8,128)(2,1)S(1)} %get-tuple-element.25, bf16[1,2048,1024]{2,1,0:T(8,128)(2,1)S(1)} %copy-done.6), kind=kOutput, calls=%fused_computation.12 | convolution fusion | flops 2149580800 | bytes 11534336 | tf_op jit(solution)/shard_map/dot_general | solution.py:268
  91.5 108.6 %shard_map.119 = (bf16[4,128,2048]{2,1,0:T(8,128)(2,1)}, bf16[4,128,2048]{2,1,0:T(8,128)(2,1)}, f32[4,8,128]{2,1,0:T(8,128)}, f32[256,1024]{1,0:T(8,128)}, f32[256,1024]{1,0:T(8,128)}, /*index=5*/f32[256,1024]{1,0:T(8,128)}) custom-call(bf16[4,128,2048]{2,1,0:T(8,128)(2,1)} %bitcast.52, bf16[4,128,2048]{2,1,0:T(8,128)(2,1)} %bitcast.53, ...), custom_call_target="tpu_custom_call" | custom-call | tf_op jit(solution)/shard_map/pallas_call | solution.py:252
  200.2 0.0 copy-start.3
  200.2 3.1 %reduce_sum.53 = bf16[128,2048]{1,0:T(8,128)(2,1)} reduce(bf16[4,128,2048]{2,1,0:T(8,128)(2,1)} %get-tuple-element.18, bf16[]{:T(256)} %constant.6.clone.1), dimensions={0}, to_apply=%region_2.3 | reduce | flops 786432 | bytes 2621442 | tf_op jit(solution)/shard_map/reduce_sum | solution.py:313
  203.2 1.3 reduce_sum.54
  204.5 0.7 slice.7
  205.3 0.6 select_reduce_fusion
  205.8 2.4 %copy.19 = f32[1,256,1024]{2,1,0:T(8,128)} copy(f32[1,256,1024]{2,1,0:T(8,128)} %bitcast.56) | data formatting | bytes 2097152
  208.2 1.0 copy.20
  209.2 1.0 copy.21
  (16 shorter events, 0.0 us)
Async XLA Ops:
  56.1 5.3 %copy-start.6 = (bf16[1,2048,1024]{2,1,0:T(8,128)(2,1)S(1)}, bf16[1,2048,1024]{2,1,0:T(8,128)(2,1)}, u32[]{:S(2)}) copy-start(bf16[1,2048,1024]{2,1,0:T(8,128)(2,1)} %param.11) | copy-start | bytes 12582916
  56.1 5.3 %copy-start.7 = (bf16[4,128,2048]{2,1,0:T(8,128)(2,1)S(1)}, bf16[4,128,2048]{2,1,0:T(8,128)(2,1)}, u32[]{:S(2)}) copy-start(bf16[4,128,2048]{2,1,0:T(8,128)(2,1)} %get-tuple-element.16) | copy-start | bytes 6291460
  61.4 2.4 %copy-start.4 = (bf16[1,2048,1024]{2,1,0:T(8,128)(2,1)S(1)}, bf16[1,2048,1024]{2,1,0:T(8,128)(2,1)}, u32[]{:S(2)}) copy-start(bf16[1,2048,1024]{2,1,0:T(8,128)(2,1)} %param.13) | copy-start | bytes 12582916
  61.4 2.9 %copy-start.8 = (bf16[4,128,2048]{2,1,0:T(8,128)(2,1)S(1)}, bf16[4,128,2048]{2,1,0:T(8,128)(2,1)}, u32[]{:S(2)}) copy-start(bf16[4,128,2048]{2,1,0:T(8,128)(2,1)} %get-tuple-element.17) | copy-start | bytes 6291460
  81.1 4.4 %copy-start.5 = (bf16[1,2048,1024]{2,1,0:T(8,128)(2,1)S(1)}, bf16[1,2048,1024]{2,1,0:T(8,128)(2,1)}, u32[]{:S(2)}) copy-start(bf16[1,2048,1024]{2,1,0:T(8,128)(2,1)} %param.12) | copy-start | bytes 12582916
  200.2 3.1 %copy-start = (bf16[4,128,2048]{2,1,0:T(8,128)(2,1)S(1)}, bf16[4,128,2048]{2,1,0:T(8,128)(2,1)}, u32[]{:S(2)}) copy-start(bf16[4,128,2048]{2,1,0:T(8,128)(2,1)} %get-tuple-element.19) | copy-start | bytes 6291460
  200.2 5.1 %copy-start.3 = (s32[128,2]{0,1:T(2,128)S(1)}, s32[128,2]{0,1:T(2,128)}, u32[]{:S(2)}) copy-start(s32[128,2]{0,1:T(2,128)} %param.9) | copy-start | bytes 3076
  203.2 5.0 %copy-start.2 = (f32[256,1024]{1,0:T(8,128)S(1)}, f32[256,1024]{1,0:T(8,128)}, u32[]{:S(2)}) copy-start(f32[256,1024]{1,0:T(8,128)} %get-tuple-element.22) | copy-start | bytes 3145732
  205.8 3.4 %copy-start.1 = (f32[256,1024]{1,0:T(8,128)S(1)}, f32[256,1024]{1,0:T(8,128)}, u32[]{:S(2)}) copy-start(f32[256,1024]{1,0:T(8,128)} %get-tuple-element.23) | copy-start | bytes 3145732
